TPU v7x, 32 devices: a whole 2x2x4 slice. The times are simulated.
32 devices in a mesh: groups: 2 (over y), expert: 16 (over z, x, core), head: 1.
Axes of the slice: x: 2, y: 2, z: 4, core: 2. Of those that a mesh axis runs over, the one named last changes fastest.
Arguments:
- sources: bfloat16 [4096, 1024], P(('groups', 'expert')), parts along dimension 0, may hold values from -6 to 6
- enc_gain: float32 [1024], replicated, may hold values from 0.1 to 1.9
- route_ids: int32 [4096, 2], P(('groups', 'expert')), parts along dimension 0, may hold values from 0 to 7, all different within a row; in each aligned block of 128 rows (0 to 127, 128 to 255, ...) at most 40 rows name the same one
- route_gates: float32 [4096, 2], P(('groups', 'expert')), parts along dimension 0, may hold values from 0.2 to 1
- w_in: bfloat16 [16, 1024, 2048], P('expert', None, 'head'), may hold values from -0.1875 to 0.1875
- w_out: bfloat16 [16, 2048, 1024], P('expert', 'head'), may hold values from -0.09375 to 0.09375
- targets: bfloat16 [4096, 1024], P(('groups', 'expert')), parts along dimension 0, may hold values from -6 to 6
- dec_gain: float32 [1024], replicated, may hold values from 0.1 to 1.9
- src_lengths: int32 [64], P(('groups', 'expert')), parts along dimension 0, may hold values from 16 to 64, as said below
- tgt_lengths: int32 [64], P(('groups', 'expert')), parts along dimension 0, may hold values from 16 to 64, as said below
- w_query: bfloat16 [1024, 1024], P('expert', 'head'), may hold values from -60 to 60
- w_key: bfloat16 [1024, 1024], P('expert', 'head'), may hold values from -0.1875 to 0.1875
- w_value: bfloat16 [1024, 1024], P('expert', 'head'), may hold values from -0.1875 to 0.1875
- w_attn: bfloat16 [1024, 1024], P('expert', 'head'), may hold values from -0.1875 to 0.1875
Outputs:
- memory: bfloat16 [4096, 1024], P(('groups', 'expert')), parts along dimension 0
- decoded: bfloat16 [4096, 1024], P(('groups', 'expert'), 'head'), parts along dimension 0
There are 2 independent parts, one for each index of `groups`. A program takes and returns all parts, laid end to end along the dimension named above; an argument that names none is the same for every part. Nothing has to cross between parts.
Inputs may be any that keep to these rules, and one draw needn't show every extreme that they name: `route_ids`: in each aligned block of 128 rows no expert is named more than 40 times, a bound that some block reaches. `src_lengths`: some sentence has exactly 64 live tokens. `tgt_lengths`: some sentence has exactly 64 live tokens.
All inputs are finite; a program needn't handle non-finite values.
Results may differ from a plain program's by a relative error of at most 0.025.
Values may be sent and summed in bfloat16 or wider, within the bound.
No kernel may reach another device: no remote copies, remote signals or barrier semaphores. Data moves between devices by JAX's collectives and lax.ppermute only.
A program may use at most 64 MiB of HBM per device.

v0:
```python
import jax
import jax.numpy as jnp
from jax import lax
from jax.sharding import PartitionSpec as P

DH = 64


def from_partner(x, axis, stride):
    return lax.ppermute(x, axis, [(i, i ^ 1 << stride) for i in range(lax.axis_size(axis))])


def layer_norm(rows, gain):
    rows = rows.astype(jnp.float32)
    mean = jnp.mean(rows, axis=-1, keepdims=True)
    centered = rows - mean
    spread = jnp.mean(centered * centered, axis=-1, keepdims=True)
    return centered * lax.rsqrt(spread + 1e-05) * gain


def partner(block):
    return from_partner(block, "expert", 0)


def shards(
    sources,
    enc_gain,
    route_ids,
    route_gates,
    w_in,
    w_out,
    targets,
    dec_gain,
    src_lengths,
    tgt_lengths,
    w_query,
    w_key,
    w_value,
    w_attn,
):
    tok_rows, width = sources.shape
    experts = lax.axis_size("expert") // 2
    capacity = 2 * ((5 * tok_rows + 4 * experts - 1) // (4 * experts))
    side = lax.axis_index("expert") % 2
    pair_ids = route_ids.reshape(-1)
    onehot = (pair_ids[:, None] == jnp.arange(experts, dtype=jnp.int32)[None, :]).astype(jnp.int32)
    earlier = jnp.cumsum(onehot, axis=0) - onehot
    slots = jnp.sum(earlier * onehot, axis=1)
    place = pair_ids * capacity + slots
    normed = layer_norm(sources, enc_gain).astype(jnp.bfloat16)
    outgoing = (
        jnp.zeros((experts * capacity, width), jnp.bfloat16)
        .at[place]
        .set(jnp.repeat(normed, 2, axis=0))
    )
    sending = outgoing.reshape(2 * experts, capacity // 2, width)
    arrived = lax.all_to_all(sending, "expert", split_axis=0, concat_axis=0, tiled=True)
    other = partner(arrived)
    lower = jnp.where(side == 0, arrived, other)
    upper = jnp.where(side == 0, other, arrived)
    arrived = jnp.concatenate((lower, upper), axis=1)
    expert_rows = arrived.reshape(-1, width)
    hidden = jnp.maximum(
        jnp.dot(expert_rows, w_in[0], preferred_element_type=jnp.float32), 0.0
    ).astype(jnp.bfloat16)
    quarter = jnp.dot(hidden, w_out[0], preferred_element_type=jnp.float32)
    half = lax.psum(quarter.astype(jnp.bfloat16), "head")
    kept = half.shape[1]
    half = half.reshape(2 * experts, capacity, kept)
    other_half = partner(half)
    merged = (half.astype(jnp.float32) + other_half.astype(jnp.float32)).astype(jnp.bfloat16)
    leaving = lax.dynamic_slice_in_dim(merged, side * (capacity // 2), capacity // 2, 1)
    returned = lax.all_to_all(leaving, "expert", split_axis=0, concat_axis=0, tiled=True)
    results = returned.reshape(-1, kept)
    picked = jnp.take(results, place, axis=0).astype(jnp.float32).reshape(tok_rows, 2, kept)
    moe = route_gates[:, 0:1] * picked[:, 0, :] + route_gates[:, 1:2] * picked[:, 1, :]
    memory = (sources.astype(jnp.float32) + moe).astype(jnp.bfloat16)
    w_q, w_k, w_v, w_o = (
        lax.all_gather(w_query, "expert", axis=0, tiled=True),
        lax.all_gather(w_key, "expert", axis=0, tiled=True),
        lax.all_gather(w_value, "expert", axis=0, tiled=True),
        lax.all_gather(w_attn, "expert", axis=0, tiled=True),
    )
    tnormed = layer_norm(targets, dec_gain).astype(jnp.bfloat16)
    query = jnp.dot(tnormed, w_q, preferred_element_type=jnp.float32).astype(jnp.bfloat16)
    key = jnp.dot(memory, w_k, preferred_element_type=jnp.float32).astype(jnp.bfloat16)
    value = jnp.dot(memory, w_v, preferred_element_type=jnp.float32).astype(jnp.bfloat16)
    sentences = src_lengths.shape[0]
    local_heads = query.shape[1] // DH
    queries = query.reshape(sentences, -1, local_heads, DH)
    keys = key.reshape(sentences, -1, local_heads, DH)
    values = value.reshape(sentences, -1, local_heads, DH)
    key_count = keys.shape[1]
    scores = jnp.einsum(
        "sqhd,skhd->shqk", queries, keys, preferred_element_type=jnp.float32
    ) * DH ** (-0.5)
    live = jnp.arange(key_count, dtype=jnp.int32)[None, :] < src_lengths[:, None]
    scores = jnp.where(live[:, None, None, :], scores, -1e30)
    top = jnp.max(scores, axis=-1, keepdims=True)
    raised = jnp.exp(scores - top)
    weights = (raised / jnp.sum(raised, axis=-1, keepdims=True)).astype(jnp.bfloat16)
    context = jnp.einsum(
        "shqk,skhd->sqhd", weights, values, preferred_element_type=jnp.float32
    ).astype(jnp.bfloat16)
    context = context.reshape(targets.shape[0], -1)
    partial_out = lax.dot_general(
        context, w_o, (((1,), (1,)), ((), ())), preferred_element_type=jnp.float32
    )
    attn = lax.psum_scatter(
        partial_out.astype(jnp.bfloat16), "head", scatter_dimension=1, tiled=True
    ).astype(jnp.float32)
    share = width // lax.axis_size("head")
    own_targets = lax.dynamic_slice_in_dim(
        targets, lax.axis_index("head") * share, share, 1
    ).astype(jnp.float32)
    per_sentence = targets.shape[0] // sentences
    positions = jnp.arange(targets.shape[0], dtype=jnp.int32)
    owner = positions // per_sentence
    live_rows = (positions % per_sentence < jnp.take(tgt_lengths, owner)).astype(jnp.float32)
    decoded = ((own_targets + attn) * live_rows[:, None]).astype(jnp.bfloat16)
    return (memory, decoded)


def solution(mesh):
    placed = (
        P(("groups", "expert"), None),
        P(),
        P(("groups", "expert"), None),
        P(("groups", "expert"), None),
        P("expert", None, "head"),
        P("expert", "head", None),
        P(("groups", "expert"), None),
        P(),
        P(("groups", "expert")),
        P(("groups", "expert")),
        P("expert", "head"),
        P("expert", "head"),
        P("expert", "head"),
        P("expert", "head"),
    )
    return jax.shard_map(
        shards,
        mesh=mesh,
        in_specs=placed,
        out_specs=(P(("groups", "expert"), None), P(("groups", "expert"), "head")),
        check_vma=False,
    )
```

profile of v0, /device:TPU:0, one launch (start us, length us, event | category | flops | bytes accessed | tf_op | source)
XLA Modules:
  0.0 201.6 jit_solution(6229918482698029241)
XLA Ops:
  7.2 0.0 all-gather.7.cloned.1.call-start
  7.2 0.7 all-gather.7.cloned.1.call-update
  7.9 0.0 all-gather.5.cloned.1.call-start
  7.9 0.7 all-gather.5.cloned.1.call-update
  8.6 0.8 copy.44
  9.4 0.1 eq.34
  9.6 0.1 reshape.203
  9.7 0.7 broadcast_multiply_fusion
  10.4 0.1 copy.47
  10.5 0.1 mul.103
  10.7 0.6 reduce-window.6
  11.3 0.2 slice_reduce_fusion
  11.5 1.1 convert_reduce_fusion.1
  12.6 1.2 fusion.27
  13.8 1.2 fusion.29
  15.0 0.3 broadcast_in_dim.50
  15.2 0.2 reshape.235
  15.4 0.1 fusion.46
  15.5 1.9 scatter_custom_fusion
  17.4 1.0 reshape.206
  18.5 7.4 %all-to-all-start = ((bf16[16,20,1024]{2,1,0:T(8,128)(2,1)}), bf16[16,20,1024]{2,1,0:T(8,128)(2,1)S(1)}, u32[]{:S(2)}, u32[]{:S(2)}) async-start(bf16[16,20,1024]{2,1,0:T(8,128)(2,1)} %reshape.206), calls=%async_computation | async-start | bytes 1572864 | tf_op jit(solution)/shard_map/all_to_all | solution.py:57
  25.8 0.0 all-gather.9.cloned.1.call-start
  25.9 0.7 all-gather.9.cloned.1.call-update
  26.6 0.0 all-gather.11.cloned.1.call-start
  26.6 19.0 %all-to-all-done = bf16[16,20,1024]{2,1,0:T(8,128)(2,1)S(1)} async-done(((bf16[16,20,1024]{2,1,0:T(8,128)(2,1)}), bf16[16,20,1024]{2,1,0:T(8,128)(2,1)S(1)}, u32[]{:S(2)}, u32[]{:S(2)}) %all-to-all-start) | async-done | bytes 655392 | tf_op jit(solution)/shard_map/all_to_all | solution.py:57
  45.6 0.4 copy.48
  46.0 0.3 collective-permute-start
  46.3 1.9 collective-permute-done
  48.2 0.4 broadcast_select_fusion.1
  48.6 0.3 pad_maximum_fusion
  48.9 9.1 %fusion.7 = bf16[640,1024]{1,0:T(8,128)(2,1)S(1)} fusion(bf16[1,2048,1024]{2,1,0:T(8,128)(2,1)} %param.19, bf16[640,1024]{1,0:T(8,128)(2,1)S(1)} %bitcast.61, bf16[1,1024,2048]{2,1,0:T(8,128)(2,1)} %param.18), kind=kOutput, calls=%fused_computation.8 | convolution fusion | flops 5371985920 | bytes 11010048 | tf_op jit(solution)/shard_map/dot_general | solution.py:66
  58.0 0.3 collective-permute-start.1
  58.4 0.6 fusion.55
  59.0 0.1 convert_reduce_fusion
  59.1 0.2 fusion.24
  59.4 1.8 collective-permute-done.1
  61.1 1.5 add_convert_fusion
  62.6 11.7 %all-to-all-start.1 = ((bf16[16,20,1024]{2,1,0:T(8,128)(2,1)}), bf16[16,20,1024]{2,1,0:T(8,128)(2,1)S(1)}, u32[]{:S(2)}, u32[]{:S(2)}) async-start(bf16[16,20,1024]{2,1,0:T(8,128)(2,1)} %add_convert_fusion), calls=%async_computation.1 | async-start | bytes 1572864 | tf_op jit(solution)/shard_map/all_to_all | solution.py:73
  74.3 1.3 compare_convert_fusion
  75.7 0.1 reduce_sum.59
  75.8 0.1 copy.46
  75.9 0.1 iota_compare_fusion.2
  76.0 2.1 %convolution_convert_fusion.3 = bf16[128,1024]{1,0:T(8,128)(2,1)S(1)} fusion(bf16[1024,1024]{1,0:T(8,128)(2,1)} %all-gather.7.cloned.1.call-done, bf16[128,1024]{1,0:T(8,128)(2,1)S(1)} %copy-done, f32[1024]{0:T(1024)S(1)} %copy-done.4, f32[128]{0:T(128)S(1)} %add_rsqrt_fusion, f32[128]{0:T(128)S(1)} %broadcast_multiply_fusion.1), kind=kOutput, calls=%fused_computation.23 | convolution fusion | flops 269221888 | bytes 2626560 | tf_op jit(solution)/shard_map/dot_general | solution.py:85
  78.1 0.3 reshape.211
  78.5 15.5 %all-to-all-done.1 = bf16[16,20,1024]{2,1,0:T(8,128)(2,1)S(1)} async-done(((bf16[16,20,1024]{2,1,0:T(8,128)(2,1)}), bf16[16,20,1024]{2,1,0:T(8,128)(2,1)S(1)}, u32[]{:S(2)}, u32[]{:S(2)}) %all-to-all-start.1) | async-done | bytes 655392 | tf_op jit(solution)/shard_map/all_to_all | solution.py:73
  94.0 0.1 reshape.209
  94.1 1.2 gather_fusion
  95.3 0.2 gather.11
  95.5 0.2 fusion.37
  95.8 0.5 copy-done.1
  96.3 0.2 fusion.30
  96.4 10.8 %all-gather.5.cloned.1.call-done = bf16[1024,1024]{1,0:T(8,128)(2,1)} async-done(((bf16[64,1024]{1,0:T(8,128)(2,1)}), bf16[1024,1024]{1,0:T(8,128)(2,1)}) %all-gather.5.cloned.1.call-update) | async-done | bytes 2097168 | tf_op jit(solution)/shard_map/all_gather | solution.py:81
  107.3 2.0 %convolution_convert_fusion.4 = bf16[128,1024]{1,0:T(8,128)(2,1)S(1)} fusion(bf16[128,1024]{1,0:T(8,128)(2,1)S(1)} %fusion.30, bf16[1024,1024]{1,0:T(8,128)(2,1)} %all-gather.5.cloned.1.call-done), kind=kOutput, calls=%fused_computation.24 | convolution fusion | flops 268566528 | bytes 2621440 | tf_op jit(solution)/shard_map/dot_general | solution.py:87
  109.3 0.3 reshape.210
  109.7 40.1 %all-gather.9.cloned.1.call-done = bf16[1024,1024]{1,0:T(8,128)(2,1)} async-done(((bf16[64,1024]{1,0:T(8,128)(2,1)}), bf16[1024,1024]{1,0:T(8,128)(2,1)}) %all-gather.9.cloned.1.call-update) | async-done | bytes 2097168 | tf_op jit(solution)/shard_map/all_gather | solution.py:80
  149.8 2.0 %convolution_convert_fusion.2 = bf16[128,1024]{1,0:T(8,128)(2,1)S(1)} fusion(bf16[128,1024]{1,0:T(8,128)(2,1)S(1)} %fusion.30, bf16[1024,1024]{1,0:T(8,128)(2,1)} %all-gather.9.cloned.1.call-done), kind=kOutput, calls=%fused_computation.22 | convolution fusion | flops 268566528 | bytes 2621440 | tf_op jit(solution)/shard_map/dot_general | solution.py:86
  151.8 0.3 reshape.212
  152.2 0.6 fusion.56
  152.7 1.4 fusion.12
  154.1 2.0 %fusion.13 = bf16[2,64,16,64]{1,3,2,0:T(8,128)(2,1)S(1)} fusion(bf16[2,64,16,64]{3,2,1,0:T(8,128)(2,1)S(1)} %reshape.210, f32[2,16,64]{2,1,0:T(8,128)S(1)} %fusion.56, f32[2,16,64,64]{2,3,1,0:T(8,128)} %fusion.12), kind=kOutput, calls=%fused_computation.16 | convolution fusion | flops 17303616 | bytes 1056768 | tf_op jit(solution)/shard_map/shqk,skhd->sqhd/dot_general | solution.py:102
  156.2 0.4 copy.56
  156.6 0.3 reshape.213
  157.0 35.0 %all-gather.11.cloned.1.call-done = bf16[1024,1024]{1,0:T(8,128)(2,1)} async-done(((bf16[64,1024]{1,0:T(8,128)(2,1)}), bf16[1024,1024]{1,0:T(8,128)(2,1)}) %all-gather.11.cloned.1.call-update) | async-done | bytes 2097168 | tf_op jit(solution)/shard_map/all_gather | solution.py:82
  192.0 3.1 %fusion.17 = bf16[128,1024]{1,0:T(8,128)(2,1)} fusion(bf16[128,1024]{1,0:T(8,128)(2,1)S(1)} %reshape.213, bf16[1024,1024]{1,0:T(8,128)(2,1)} %all-gather.11.cloned.1.call-done, bf16[128,1024]{1,0:T(8,128)(2,1)S(1)} %copy-done, f32[128]{0:T(128)S(1)} %compare_convert_fusion), kind=kOutput, calls=%fused_computation.21 | convolution fusion | flops 269221888 | bytes 2884096 | tf_op jit(solution)/shard_map/dot_general | solution.py:106
  (28 shorter events, 0.2 us)
Async XLA Ops:
  7.2 68.9 %all-gather.7.cloned.1.call-start = ((), (), s32[]{:S(2)}) async-start(), calls=%async_computation.3 | async-start | bytes 2228224 | tf_op jit(solution)/shard_map/all_gather | solution.py:79
  7.9 99.4 %all-gather.5.cloned.1.call-start = ((), (), s32[]{:S(2)}) async-start(), calls=%async_computation.2 | async-start | bytes 2228224 | tf_op jit(solution)/shard_map/all_gather | solution.py:81
  18.5 27.2 %all-to-all-start = ((bf16[16,20,1024]{2,1,0:T(8,128)(2,1)}), bf16[16,20,1024]{2,1,0:T(8,128)(2,1)S(1)}, u32[]{:S(2)}, u32[]{:S(2)}) async-start(bf16[16,20,1024]{2,1,0:T(8,128)(2,1)} %reshape.206), calls=%async_computation | async-start | bytes 1572864 | tf_op jit(solution)/shard_map/all_to_all | solution.py:57
  25.8 123.9 %all-gather.9.cloned.1.call-start = ((), (), s32[]{:S(2)}) async-start(), calls=%async_computation.4 | async-start | bytes 2228224 | tf_op jit(solution)/shard_map/all_gather | solution.py:80
  26.6 165.4 %all-gather.11.cloned.1.call-start = ((), (), s32[]{:S(2)}) async-start(), calls=%async_computation.5 | async-start | bytes 2228224 | tf_op jit(solution)/shard_map/all_gather | solution.py:82
  46.0 2.2 %collective-permute-start = (bf16[16,20,1024]{2,0,1:T(8,128)(2,1)S(1)}, bf16[16,20,1024]{2,0,1:T(8,128)(2,1)S(1)}, u32[]{:S(2)}, u32[]{:S(2)}) collective-permute-start(bf16[16,20,1024]{2,0,1:T(8,128)(2,1)S(1)} %copy.48), channel_id=1, source_target_pairs={{0,1},{1,0},{2,3},{3,2},{4,5},{5,4},{6,7},{7,6},{8,9},{9,8},{10,11... | collective-permute-start | bytes 1966088 | tf_op jit(solution)/shard_map/ppermute | solution.py:10
  48.9 9.5 %copy-start.5 = (s32[2]{0:T(128)S(1)}, s32[2]{0:T(128)}, u32[]{:S(2)}) copy-start(s32[2]{0:T(128)} %param.23) | copy-start | bytes 28
  48.9 10.1 %copy-start = (bf16[128,1024]{1,0:T(8,128)(2,1)S(1)}, bf16[128,1024]{1,0:T(8,128)(2,1)}, u32[]{:S(2)}) copy-start(bf16[128,1024]{1,0:T(8,128)(2,1)} %param.20) | copy-start | bytes 786436
  58.0 3.1 %collective-permute-start.1 = (bf16[16,40,1024]{2,1,0:T(8,128)(2,1)S(1)}, bf16[16,40,1024]{2,1,0:T(8,128)(2,1)S(1)}, u32[]{:S(2)}, u32[]{:S(2)}) collective-permute-start(bf16[16,40,1024]{2,1,0:T(8,128)(2,1)S(1)} %bitcast.62), channel_id=1, source_target_pairs={{0,1},{1,0},{2,3},{3,2},{4,5},{5,4},{6,7},{7,6},{8,9},{9,8},{10,11... | collective-permute-start | bytes 3932168 | tf_op jit(solution)/shard_map/ppermute | solution.py:10
  59.3 16.6 %copy-start.7 = (s32[2]{0:T(128)S(1)}, s32[2]{0:T(128)}, u32[]{:S(2)}) copy-start(s32[2]{0:T(128)} %param.22) | copy-start | bytes 28
  59.3 16.6 %copy-start.6 = (f32[128,2]{0,1:T(2,128)S(1)}, f32[128,2]{0,1:T(2,128)}, u32[]{:S(2)}) copy-start(f32[128,2]{0,1:T(2,128)} %param.17) | copy-start | bytes 3076
  59.3 16.6 %copy-start.3 = (s32[128,2]{0,1:T(2,128)S(1)}, s32[128,2]{0,1:T(2,128)}, u32[]{:S(2)}) copy-start(s32[128,2]{0,1:T(2,128)} %param.16) | copy-start | bytes 3076
  59.3 16.7 %copy-start.4 = (f32[1024]{0:T(1024)S(1)}, f32[1024]{0:T(1024)}, u32[]{:S(2)}) copy-start(f32[1024]{0:T(1024)} %param.21) | copy-start | bytes 12292
  62.6 31.4 %all-to-all-start.1 = ((bf16[16,20,1024]{2,1,0:T(8,128)(2,1)}), bf16[16,20,1024]{2,1,0:T(8,128)(2,1)S(1)}, u32[]{:S(2)}, u32[]{:S(2)}) async-start(bf16[16,20,1024]{2,1,0:T(8,128)(2,1)} %add_convert_fusion), calls=%async_computation.1 | async-start | bytes 1572864 | tf_op jit(solution)/shard_map/all_to_all | solution.py:73
  95.3 1.0 copy-start.1
  96.4 55.4 %copy-start.2 = (bf16[128,1024]{1,0:T(8,128)(2,1)}, bf16[128,1024]{1,0:T(8,128)(2,1)S(1)}, u32[]{:S(2)}) copy-start(bf16[128,1024]{1,0:T(8,128)(2,1)S(1)} %fusion.30) | copy-start | bytes 786436
Sparse Core Ops, SparseCore 0:
  10.2 49.3 all-gather.6
  61.7 45.5 all-gather.4
  109.4 40.2 all-gather.8
  151.8 40.1 all-gather.10
where the time goes:
time: 202 us
  waiting for transfers between devices  126 us (62%)
  matrix products  22.4 us (11%)
  starting transfers between devices  19.8 us (10%)
  between operations  14.1 us (7%)
  local copies, waits for them, and re-layouts  9.9 us (5%)
  other arithmetic  9.17 us (5%)
    all_gather x1, waiting for transfers between devices, shards(): lax.all_gather(w_key, 'expert', axis=0, tiled=True)  40.1 us
    all_gather x1, waiting for transfers between devices, shards(): lax.all_gather(w_attn, 'expert', axis=0, tiled=True)  35 us
    all_to_all x1, waiting for transfers between devices, shards(): lax.all_to_all(sending, 'expert', split_axis=0, concat_axis=0, tiled=True)  19 us
    all_to_all x1, waiting for transfers between devices, shards(): lax.all_to_all(leaving, 'expert', split_axis=0, concat_axis=0, tiled=True)  15.5 us
    all_to_all x1, starting transfers between devices, shards(): lax.all_to_all(leaving, 'expert', split_axis=0, concat_axis=0, tiled=True)  11.7 us
    all_gather x1, waiting for transfers between devices, shards(): lax.all_gather(w_value, 'expert', axis=0, tiled=True)  10.8 us
    dot_general x1, matrix products, shards(): quarter = jnp.dot(hidden, w_out[0], preferred_element_type=jnp.float32)  9.11 us
    all_to_all x1, starting transfers between devices, shards(): lax.all_to_all(sending, 'expert', split_axis=0, concat_axis=0, tiled=True)  7.36 us
  transfers between devices with their start and end apart: 8, of which 7 were waited for; matrix products, arithmetic and copies ran while one was open for 19% of the time, Pallas kernels for 0%

commit v1 on v0

--- a/solution.py
+++ b/solution.py
@@ -4,6 +4,27 @@
 from jax.sharding import PartitionSpec as P
 
 DH = 64
+
+
+def laid_out(blocks, dim):
+    lengths = list(blocks.shape[1:])
+    lengths[dim] *= blocks.shape[0]
+    return jnp.moveaxis(blocks, 0, dim).reshape(lengths)
+
+
+def collected_by_bits(x, axis):
+    size, index = (lax.axis_size(axis), lax.axis_index(axis))
+    blocks, distance = (x[None], 1)
+    while distance < size:
+        other = lax.ppermute(blocks, axis, [(i, i ^ distance) for i in range(size)])
+        low = index & distance == 0
+        blocks = jnp.concatenate([jnp.where(low, blocks, other), jnp.where(low, other, blocks)])
+        distance *= 2
+    return blocks
+
+
+def gather_by_bits(x, axis, dim):
+    return laid_out(collected_by_bits(x, axis), dim)
 
 
 def from_partner(x, axis, stride):
@@ -79,7 +100,7 @@
         lax.all_gather(w_query, "expert", axis=0, tiled=True),
         lax.all_gather(w_key, "expert", axis=0, tiled=True),
         lax.all_gather(w_value, "expert", axis=0, tiled=True),
-        lax.all_gather(w_attn, "expert", axis=0, tiled=True),
+        gather_by_bits(w_attn, "expert", 0),
     )
     tnormed = layer_norm(targets, dec_gain).astype(jnp.bfloat16)
     query = jnp.dot(tnormed, w_q, preferred_element_type=jnp.float32).astype(jnp.bfloat16)

time: 202 us -> 191 us (0.946)
  waiting for transfers between devices: 126 us -> 93 us
  starting transfers between devices: 19.8 us -> 28.8 us
  other arithmetic: 9.17 us -> 15.4 us
  local copies, waits for them, and re-layouts: 9.9 us -> 14.4 us
  matrix products: 22.4 us -> 24.9 us
    ppermute x0 -> x4, waiting for transfers between devices: none -> 62.8 us  [collected_by_bits(): other = lax.ppermute(blocks, axis, [(i, i ^ distance) for i in range(size)])]
    all_gather x1, waiting for transfers between devices: 40.1 us -> 0.02 us  [shards(): lax.all_gather(w_key, 'expert', axis=0, tiled=True)]
    all_gather x1 -> x0, waiting for transfers between devices: 35 us -> none  [shards(): lax.all_gather(w_attn, 'expert', axis=0, tiled=True)]
    ppermute x0 -> x4, starting transfers between devices: none -> 16.2 us  [collected_by_bits(): other = lax.ppermute(blocks, axis, [(i, i ^ distance) for i in range(size)])]
    all_to_all x1, waiting for transfers between devices: 15.5 us -> 3.67 us  [shards(): lax.all_to_all(leaving, 'expert', split_axis=0, concat_axis=0, tiled=True)]
    all_to_all x1, starting transfers between devices: 11.7 us -> 4.46 us  [shards(): lax.all_to_all(leaving, 'expert', split_axis=0, concat_axis=0, tiled=True)]
    all_gather x1, waiting for transfers between devices: 10.8 us -> 6.87 us  [shards(): lax.all_gather(w_value, 'expert', axis=0, tiled=True)]
    ppermute x2, waiting for transfers between devices: 3.64 us -> 0.01 us  [from_partner(): lax.ppermute(x, axis, [(i, i ^ 1 << stride) for i in range(lax.axis_size(...]
  transfers between devices with their start and end apart: 8 -> 11, of which waited for: 7 -> 7; matrix products, arithmetic and copies ran while one was open for 19% -> 24% of each run, Pallas kernels for 0% -> 0%
where the time goes in v1:
time: 191 us
  waiting for transfers between devices  93 us (49%)
  starting transfers between devices  28.8 us (15%)
  matrix products  24.9 us (13%)
  other arithmetic  15.4 us (8%)
  local copies, waits for them, and re-layouts  14.4 us (8%)
  between operations  14.1 us (7%)
    ppermute x4, waiting for transfers between devices, collected_by_bits(): other = lax.ppermute(blocks, axis, [(i, i ^ distance) for i in range(size)])  62.8 us
    all_to_all x1, waiting for transfers between devices, shards(): lax.all_to_all(sending, 'expert', split_axis=0, concat_axis=0, tiled=True)  18.1 us
    ppermute x4, starting transfers between devices, collected_by_bits(): other = lax.ppermute(blocks, axis, [(i, i ^ distance) for i in range(size)])  16.2 us
    dot_general x1, matrix products, shards(): quarter = jnp.dot(hidden, w_out[0], preferred_element_type=jnp.float32)  10.1 us
    all_to_all x1, starting transfers between devices, shards(): lax.all_to_all(sending, 'expert', split_axis=0, concat_axis=0, tiled=True)  7.49 us
    all_gather x1, waiting for transfers between devices, shards(): lax.all_gather(w_value, 'expert', axis=0, tiled=True)  6.87 us
    all_to_all x1, starting transfers between devices, shards(): lax.all_to_all(leaving, 'expert', split_axis=0, concat_axis=0, tiled=True)  4.46 us
  transfers between devices with their start and end apart: 11, of which 7 were waited for; matrix products, arithmetic and copies ran while one was open for 24% of the time, Pallas kernels for 0%

profile of v1, /device:TPU:0, one launch (start us, length us, event | category | flops | bytes accessed | tf_op | source)
XLA Modules:
  0.0 190.6 jit_solution(14941596026519301896)
XLA Ops:
  7.2 0.7 all-gather.6.cloned.1.call-update
  7.9 0.7 all-gather.8.cloned.1.call-update
  8.6 0.8 copy.44
  9.4 0.1 eq.46
  9.6 0.1 reshape.206
  9.7 0.7 broadcast_multiply_fusion
  10.4 0.1 copy.47
  10.5 0.1 mul.103
  10.7 0.6 reduce-window.6
  11.3 0.2 slice_reduce_fusion
  11.5 1.1 convert_reduce_fusion.1
  12.6 1.2 fusion.27
  13.8 1.2 fusion.29
  15.0 0.3 broadcast_in_dim.53
  15.2 0.2 reshape.239
  15.6 1.9 scatter_custom_fusion
  17.4 1.0 reshape.209
  18.4 7.5 %all-to-all-start = ((bf16[16,20,1024]{2,1,0:T(8,128)(2,1)}), bf16[16,20,1024]{2,1,0:T(8,128)(2,1)S(1)}, u32[]{:S(2)}, u32[]{:S(2)}) async-start(bf16[16,20,1024]{2,1,0:T(8,128)(2,1)} %reshape.209), calls=%async_computation | async-start | bytes 1572864 | tf_op jit(solution)/shard_map/all_to_all | solution.py:78
  26.0 0.5 collective-permute-start.2
  26.5 1.0 collective-permute-done.2
  27.5 18.1 %all-to-all-done = bf16[16,20,1024]{2,1,0:T(8,128)(2,1)S(1)} async-done(((bf16[16,20,1024]{2,1,0:T(8,128)(2,1)}), bf16[16,20,1024]{2,1,0:T(8,128)(2,1)S(1)}, u32[]{:S(2)}, u32[]{:S(2)}) %all-to-all-start) | async-done | bytes 655392 | tf_op jit(solution)/shard_map/all_to_all | solution.py:78
  45.6 0.4 copy.48
  46.0 0.4 collective-permute-start
  46.5 4.3 %collective-permute-start.3 = (bf16[2,64,1024]{2,1,0:T(8,128)(2,1)S(1)}, bf16[2,64,1024]{2,1,0:T(8,128)(2,1)S(1)}, u32[]{:S(2)}, u32[]{:S(2)}) collective-permute-start(bf16[2,64,1024]{2,1,0:T(8,128)(2,1)S(1)} %pad_maximum_fusion.4), channel_id=1, source_target_pairs={{0,2},{1,3},{2,0},{3,1},{4,6},{5,7},{6,4},{7,5},{8,10},{9,11},{10,... | collective-permute-start | bytes 786440 | tf_op jit(solution)/shard_map/ppermute | solution.py:19
  50.8 0.1 convert_reduce_fusion
  50.9 6.3 %collective-permute-done.3 = bf16[2,64,1024]{2,1,0:T(8,128)(2,1)S(1)} collective-permute-done((bf16[2,64,1024]{2,1,0:T(8,128)(2,1)S(1)}, bf16[2,64,1024]{2,1,0:T(8,128)(2,1)S(1)}, u32[]{:S(2)}, u32[]{:S(2)}) %collective-permute-start.3) | collective-permute-done | bytes 262176 | tf_op jit(solution)/shard_map/ppermute | solution.py:19
  57.3 0.9 pad_maximum_fusion.3
  58.2 5.6 %collective-permute-start.4 = (bf16[4,64,1024]{2,1,0:T(8,128)(2,1)}, bf16[4,64,1024]{2,1,0:T(8,128)(2,1)}, u32[]{:S(2)}, u32[]{:S(2)}) collective-permute-start(bf16[4,64,1024]{2,1,0:T(8,128)(2,1)} %pad_maximum_fusion.3), channel_id=1, source_target_pairs={{0,4},{1,5},{2,6},{3,7},{4,0},{5,1},{6,2},{7,3},{8,12},{9,13},{10,... | collective-permute-start | bytes 1572872 | tf_op jit(solution)/shard_map/ppermute | solution.py:19
  63.7 0.4 broadcast_select_fusion.3
  64.1 0.3 pad_maximum_fusion.1
  64.4 10.1 %fusion.7 = bf16[640,1024]{1,0:T(8,128)(2,1)} fusion(bf16[1,2048,1024]{2,1,0:T(8,128)(2,1)} %param.19, bf16[640,1024]{1,0:T(8,128)(2,1)S(1)} %bitcast.66, bf16[1,1024,2048]{2,1,0:T(8,128)(2,1)} %param.18), kind=kOutput, calls=%fused_computation.9 | convolution fusion | flops 5371985920 | bytes 11010048 | tf_op jit(solution)/shard_map/dot_general | solution.py:87
  74.6 0.2 fusion.24
  74.8 3.5 %collective-permute-done.4 = bf16[4,64,1024]{2,1,0:T(8,128)(2,1)} collective-permute-done((bf16[4,64,1024]{2,1,0:T(8,128)(2,1)}, bf16[4,64,1024]{2,1,0:T(8,128)(2,1)}, u32[]{:S(2)}, u32[]{:S(2)}) %collective-permute-start.4) | collective-permute-done | bytes 524320 | tf_op jit(solution)/shard_map/ppermute | solution.py:19
  78.4 1.1 broadcast_select_fusion.5
  79.6 6.0 %collective-permute-start.5 = (bf16[8,64,1024]{2,1,0:T(8,128)(2,1)S(1)}, bf16[8,64,1024]{2,1,0:T(8,128)(2,1)S(1)}, u32[]{:S(2)}, u32[]{:S(2)}) collective-permute-start(bf16[8,64,1024]{2,1,0:T(8,128)(2,1)S(1)} %pad_maximum_fusion.2), channel_id=1, source_target_pairs={{0,8},{1,9},{2,10},{3,11},{4,12},{5,13},{6,14},{7,15},{8,0},{9,1},... | collective-permute-start | bytes 3145736 | tf_op jit(solution)/shard_map/ppermute | solution.py:19
  85.6 0.6 fusion.55
  86.2 0.6 iota_compare_fusion.2
  86.8 3.0 %add_convert_fusion = bf16[16,20,1024]{2,1,0:T(8,128)(2,1)} fusion(bf16[16,40,1024]{2,1,0:T(8,128)(2,1)} %collective-permute-done.1, s32[]{:T(128)S(6)} %select_n.159, bf16[16,40,1024]{2,1,0:T(8,128)(2,1)} %bitcast.68), kind=kLoop, calls=%fused_computation.10 | loop fusion | flops 1310720 | bytes 1966084 | tf_op jit(solution)/shard_map/convert_element_type | solution.py:92
  89.8 4.5 %all-to-all-start.1 = ((bf16[16,20,1024]{2,1,0:T(8,128)(2,1)}), bf16[16,20,1024]{2,1,0:T(8,128)(2,1)}, u32[]{:S(2)}, u32[]{:S(2)}) async-start(bf16[16,20,1024]{2,1,0:T(8,128)(2,1)} %add_convert_fusion), calls=%async_computation.1 | async-start | bytes 1572864 | tf_op jit(solution)/shard_map/all_to_all | solution.py:94
  94.3 1.9 %compare_convert_fusion = f32[128]{0:T(128)} fusion(s32[]{:T(128)} %bitcast.16, s32[]{:T(128)} %bitcast.15), kind=kLoop, calls=%fused_computation.85 | loop fusion | flops 4352 | bytes 520 | tf_op jit(solution)/shard_map/convert_element_type | solution.py:140
  96.2 0.1 reduce_sum.59
  96.4 52.0 %collective-permute-done.5 = bf16[8,64,1024]{2,1,0:T(8,128)(2,1)S(1)} collective-permute-done((bf16[8,64,1024]{2,1,0:T(8,128)(2,1)S(1)}, bf16[8,64,1024]{2,1,0:T(8,128)(2,1)S(1)}, u32[]{:S(2)}, u32[]{:S(2)}) %collective-permute-start.5) | collective-permute-done | bytes 1048608 | tf_op jit(solution)/shard_map/ppermute | solution.py:19
  148.4 0.1 broadcast_select_fusion.1
  148.6 0.2 pad_maximum_fusion
  148.8 0.5 copy-done.6
  149.3 2.1 %convolution_convert_fusion.3 = bf16[128,1024]{1,0:T(8,128)(2,1)S(1)} fusion(bf16[1024,1024]{1,0:T(8,128)(2,1)} %all-gather.6.cloned.1.call-done, bf16[128,1024]{1,0:T(8,128)(2,1)S(1)} %copy-done, f32[1024]{0:T(1024)S(1)} %copy-done.6, f32[128]{0:T(128)S(1)} %add_rsqrt_fusion, f32[128]{0:T(128)S(1)} %broadcast_multiply_fusion.1), kind=kOutput, calls=%fused_computation.24 | convolution fusion | flops 269221888 | bytes 2626560 | tf_op jit(solution)/shard_map/dot_general | solution.py:106
  151.4 1.1 reshape.214
  152.5 3.7 %all-to-all-done.1 = bf16[16,20,1024]{2,1,0:T(8,128)(2,1)} async-done(((bf16[16,20,1024]{2,1,0:T(8,128)(2,1)}), bf16[16,20,1024]{2,1,0:T(8,128)(2,1)}, u32[]{:S(2)}, u32[]{:S(2)}) %all-to-all-start.1) | async-done | bytes 655392 | tf_op jit(solution)/shard_map/all_to_all | solution.py:94
  156.2 1.2 reshape.212
  157.4 1.2 gather_fusion
  158.6 1.0 gather.11
  159.6 1.3 fusion.37
  160.9 0.2 fusion.30
  161.1 2.2 %convolution_convert_fusion.2 = bf16[128,1024]{1,0:T(8,128)(2,1)S(1)} fusion(bf16[128,1024]{1,0:T(8,128)(2,1)S(1)} %fusion.30, bf16[1024,1024]{1,0:T(8,128)(2,1)} %all-gather.8.cloned.1.call-done), kind=kOutput, calls=%fused_computation.23 | convolution fusion | flops 268566528 | bytes 2621440 | tf_op jit(solution)/shard_map/dot_general | solution.py:107
  163.3 1.1 reshape.215
  164.4 1.6 fusion.56
  166.1 2.5 %fusion.12 = f32[2,16,64,64]{2,3,1,0:T(8,128)} fusion(bf16[2,64,16,64]{3,2,1,0:T(8,128)(2,1)} %reshape.215, bf16[2,64,16,64]{3,2,1,0:T(8,128)(2,1)S(1)} %copy-done.3, pred[2,64]{1,0:T(4,128)(4,1)S(1)} %copy-done.11), kind=kOutput, calls=%fused_computation.14 | convolution fusion | flops 17039360 | bytes 1048704 | tf_op jit(solution)/shard_map/sqhd,skhd->shqk/dot_general | solution.py:115
  168.5 6.9 %all-gather.4.cloned.1.call-done = bf16[1024,1024]{1,0:T(8,128)(2,1)} async-done(((bf16[64,1024]{1,0:T(8,128)(2,1)}), bf16[1024,1024]{1,0:T(8,128)(2,1)}) %all-gather.4.cloned.1.call-update) | async-done | bytes 2097168 | tf_op jit(solution)/shard_map/all_gather | solution.py:102
  175.4 2.0 %convolution_convert_fusion.4 = bf16[128,1024]{1,0:T(8,128)(2,1)S(1)} fusion(bf16[128,1024]{1,0:T(8,128)(2,1)S(1)} %fusion.30, bf16[1024,1024]{1,0:T(8,128)(2,1)} %all-gather.4.cloned.1.call-done), kind=kOutput, calls=%fused_computation.25 | convolution fusion | flops 268566528 | bytes 2621440 | tf_op jit(solution)/shard_map/dot_general | solution.py:108
  177.4 0.3 reshape.213
  177.8 2.9 %fusion.13 = bf16[2,64,16,64]{1,3,2,0:T(8,128)(2,1)} fusion(bf16[2,64,16,64]{3,2,1,0:T(8,128)(2,1)S(1)} %reshape.213, f32[2,16,64]{2,1,0:T(8,128)S(1)} %fusion.56, f32[2,16,64,64]{2,3,1,0:T(8,128)} %fusion.12), kind=kOutput, calls=%fused_computation.17 | convolution fusion | flops 17303616 | bytes 1056768 | tf_op jit(solution)/shard_map/shqk,skhd->sqhd/dot_general | solution.py:123
  180.7 1.5 copy.56
  182.1 0.3 reshape.216
  182.5 1.5 fusion.17
  (49 shorter events, 0.7 us)
Async XLA Ops:
  7.2 141.6 %all-gather.6.cloned.1.call-start = ((), (), s32[]{:S(2)}) async-start(), calls=%async_computation.3 | async-start | bytes 2228224 | tf_op jit(solution)/shard_map/all_gather | solution.py:100
  7.9 153.2 %all-gather.8.cloned.1.call-start = ((), (), s32[]{:S(2)}) async-start(), calls=%async_computation.4 | async-start | bytes 2228224 | tf_op jit(solution)/shard_map/all_gather | solution.py:101
  15.4 10.5 %copy-start.4 = (bf16[64,1024]{1,0:T(8,128)(2,1)S(1)}, bf16[64,1024]{1,0:T(8,128)(2,1)}, u32[]{:S(2)}) copy-start(bf16[64,1024]{1,0:T(8,128)(2,1)} %param.27) | copy-start | bytes 393220
  18.4 32.3 %copy-start = (bf16[128,1024]{1,0:T(8,128)(2,1)S(1)}, bf16[128,1024]{1,0:T(8,128)(2,1)}, u32[]{:S(2)}) copy-start(bf16[128,1024]{1,0:T(8,128)(2,1)} %param.20) | copy-start | bytes 786436
  18.4 27.2 %all-to-all-start = ((bf16[16,20,1024]{2,1,0:T(8,128)(2,1)}), bf16[16,20,1024]{2,1,0:T(8,128)(2,1)S(1)}, u32[]{:S(2)}, u32[]{:S(2)}) async-start(bf16[16,20,1024]{2,1,0:T(8,128)(2,1)} %reshape.209), calls=%async_computation | async-start | bytes 1572864 | tf_op jit(solution)/shard_map/all_to_all | solution.py:78
  25.9 149.4 %all-gather.4.cloned.1.call-start = ((), (), s32[]{:S(2)}) async-start(), calls=%async_computation.2 | async-start | bytes 2228224 | tf_op jit(solution)/shard_map/all_gather | solution.py:102
  26.0 1.5 collective-permute-start.2
  46.0 17.7 %collective-permute-start = (bf16[16,20,1024]{2,0,1:T(8,128)(2,1)S(1)}, bf16[16,20,1024]{2,0,1:T(8,128)(2,1)S(1)}, u32[]{:S(2)}, u32[]{:S(2)}) collective-permute-start(bf16[16,20,1024]{2,0,1:T(8,128)(2,1)S(1)} %copy.48), channel_id=1, source_target_pairs={{0,1},{1,0},{2,3},{3,2},{4,5},{5,4},{6,7},{7,6},{8,9},{9,8},{10,11... | collective-permute-start | bytes 1966088 | tf_op jit(solution)/shard_map/ppermute | solution.py:31
  46.5 10.8 %collective-permute-start.3 = (bf16[2,64,1024]{2,1,0:T(8,128)(2,1)S(1)}, bf16[2,64,1024]{2,1,0:T(8,128)(2,1)S(1)}, u32[]{:S(2)}, u32[]{:S(2)}) collective-permute-start(bf16[2,64,1024]{2,1,0:T(8,128)(2,1)S(1)} %pad_maximum_fusion.4), channel_id=1, source_target_pairs={{0,2},{1,3},{2,0},{3,1},{4,6},{5,7},{6,4},{7,5},{8,10},{9,11},{10,... | collective-permute-start | bytes 786440 | tf_op jit(solution)/shard_map/ppermute | solution.py:19
  58.2 20.2 %collective-permute-start.4 = (bf16[4,64,1024]{2,1,0:T(8,128)(2,1)}, bf16[4,64,1024]{2,1,0:T(8,128)(2,1)}, u32[]{:S(2)}, u32[]{:S(2)}) collective-permute-start(bf16[4,64,1024]{2,1,0:T(8,128)(2,1)} %pad_maximum_fusion.3), channel_id=1, source_target_pairs={{0,4},{1,5},{2,6},{3,7},{4,0},{5,1},{6,2},{7,3},{8,12},{9,13},{10,... | collective-permute-start | bytes 1572872 | tf_op jit(solution)/shard_map/ppermute | solution.py:19
  74.6 12.2 %collective-permute-start.1 = (bf16[16,40,1024]{2,1,0:T(8,128)(2,1)}, bf16[16,40,1024]{2,1,0:T(8,128)(2,1)}, u32[]{:S(2)}, u32[]{:S(2)}) collective-permute-start(bf16[16,40,1024]{2,1,0:T(8,128)(2,1)} %bitcast.67), channel_id=1, source_target_pairs={{0,1},{1,0},{2,3},{3,2},{4,5},{5,4},{6,7},{7,6},{8,9},{9,8},{10,11... | collective-permute-start | bytes 3932168 | tf_op jit(solution)/shard_map/ppermute | solution.py:31
  74.8 10.8 %copy-start.7 = (s32[2]{0:T(128)S(1)}, s32[2]{0:T(128)}, u32[]{:S(2)}) copy-start(s32[2]{0:T(128)} %param.23) | copy-start | bytes 28
  74.8 11.4 %copy-start.10 = (s32[2]{0:T(128)S(1)}, s32[2]{0:T(128)}, u32[]{:S(2)}) copy-start(s32[2]{0:T(128)} %param.22) | copy-start | bytes 28
  79.6 16.8 %copy-start.8 = (f32[128,2]{0,1:T(2,128)S(1)}, f32[128,2]{0,1:T(2,128)}, u32[]{:S(2)}) copy-start(f32[128,2]{0,1:T(2,128)} %param.17) | copy-start | bytes 3076
  79.6 16.8 %copy-start.5 = (s32[128,2]{0,1:T(2,128)S(1)}, s32[128,2]{0,1:T(2,128)}, u32[]{:S(2)}) copy-start(s32[128,2]{0,1:T(2,128)} %param.16) | copy-start | bytes 3076
  79.6 68.8 %collective-permute-start.5 = (bf16[8,64,1024]{2,1,0:T(8,128)(2,1)S(1)}, bf16[8,64,1024]{2,1,0:T(8,128)(2,1)S(1)}, u32[]{:S(2)}, u32[]{:S(2)}) collective-permute-start(bf16[8,64,1024]{2,1,0:T(8,128)(2,1)S(1)} %pad_maximum_fusion.2), channel_id=1, source_target_pairs={{0,8},{1,9},{2,10},{3,11},{4,12},{5,13},{6,14},{7,15},{8,0},{9,1},... | collective-permute-start | bytes 3145736 | tf_op jit(solution)/shard_map/ppermute | solution.py:19
  89.8 66.4 %all-to-all-start.1 = ((bf16[16,20,1024]{2,1,0:T(8,128)(2,1)}), bf16[16,20,1024]{2,1,0:T(8,128)(2,1)}, u32[]{:S(2)}, u32[]{:S(2)}) async-start(bf16[16,20,1024]{2,1,0:T(8,128)(2,1)} %add_convert_fusion), calls=%async_computation.1 | async-start | bytes 1572864 | tf_op jit(solution)/shard_map/all_to_all | solution.py:94
  148.6 0.7 copy-start.6
  158.6 2.3 %copy-start.1 = (bf16[128,1024]{1,0:T(8,128)(2,1)S(1)}, bf16[128,1024]{1,0:T(8,128)(2,1)}, u32[]{:S(2)}) copy-start(bf16[128,1024]{1,0:T(8,128)(2,1)} %param.14) | copy-start | bytes 786436
  161.0 14.3 %copy-start.2 = (bf16[128,1024]{1,0:T(8,128)(2,1)}, bf16[128,1024]{1,0:T(8,128)(2,1)S(1)}, u32[]{:S(2)}) copy-start(bf16[128,1024]{1,0:T(8,128)(2,1)S(1)} %fusion.30) | copy-start | bytes 786436
  161.1 3.4 %copy-start.3 = (bf16[2,64,16,64]{3,2,1,0:T(8,128)(2,1)S(1)}, bf16[2,64,16,64]{3,2,1,0:T(8,128)(2,1)}, u32[]{:S(2)}) copy-start(bf16[2,64,16,64]{3,2,1,0:T(8,128)(2,1)} %reshape.214) | copy-start | bytes 786436
  161.1 3.3 %copy-start.11 = (pred[2,64]{1,0:T(4,128)(4,1)S(1)}, pred[2,64]{1,0:T(4,128)(4,1)}, u32[]{:S(2)}) copy-start(pred[2,64]{1,0:T(4,128)(4,1)} %iota_compare_fusion.2) | copy-start | bytes 388
  177.8 4.7 %copy-start.9 = (f32[128]{0:T(128)S(1)}, f32[128]{0:T(128)}, u32[]{:S(2)}) copy-start(f32[128]{0:T(128)} %compare_convert_fusion) | copy-start | bytes 1540
Sparse Core Ops, SparseCore 0:
  10.2 49.2 all-gather.5
  61.7 68.4 all-gather.7
  132.3 43.0 all-gather.3
